TPU v7x, 768 devices: a whole 4x8x12 slice. The times are simulated.
768 devices in a mesh: wide: 64 (over y, x, core), narrow: 12 (over z).
Axes of the slice: x: 4, y: 8, z: 12, core: 2. Of those that a mesh axis runs over, the one named last changes fastest.
Arguments:
- features: bfloat16 [393216, 1024], P(('wide', 'narrow')), may hold values from -6 to 6
- stale_store: bfloat16 [196608, 1024], P(('wide', 'narrow')), may hold values from -6 to 6
- serve_rows: int32 [49152, 8], P(('wide', 'narrow')), may hold values from 0 to 255
- neighbours: int32 [393216, 8], P(('wide', 'narrow')), may hold values from 0 to 1023
- degrees: int32 [393216], P(('wide', 'narrow')), may hold values from 1 to 8
- push_rows: int32 [196608], P(('wide', 'narrow')), may hold values from 0 to 511
- weight: bfloat16 [1024, 1024], replicated, may hold values from -0.1875 to 0.1875
- cotangent: bfloat16 [393216, 1024], P(('wide', 'narrow')), may hold values from -6 to 6
Outputs:
- refreshed_store: bfloat16 [196608, 1024], P(('wide', 'narrow'))
- grad_weight: float32 [1024, 1024], P('wide')
Inputs may be any that keep to these rules, and one draw needn't show every extreme that they name: `serve_rows`: A row number within the owner device's store rows. `neighbours`: A value below 512 names a node of the same device; 512 + p * 8 + q names slot q of the block pulled from partition p. Only the first degrees entries of a node are read. `push_rows`: A node of the same device.
All inputs are finite; a program needn't handle non-finite values.
Results may differ from a plain program's by a relative error of at most 0.0053.
Values may be sent and summed in bfloat16 or wider, within the bound.
A program may use at most 64 MiB of HBM per device.

v0:
```python
import math

import jax
import jax.numpy as jnp
from jax import lax
from jax.sharding import PartitionSpec as P


def local(features, stale_store, serve_rows, neighbours, degrees, push_rows, weight, cotangent):
    wide_size = lax.axis_size("wide")
    narrow_size = lax.axis_size("narrow")
    row_total = features.shape[0]
    width = features.shape[1]
    pull_slots = serve_rows.shape[1]
    outgoing = jnp.take(stale_store, serve_rows.reshape(-1), axis=0).reshape(
        wide_size, pull_slots, width
    )
    pulled = lax.all_to_all(outgoing, "wide", split_axis=0, concat_axis=0, tiled=True)
    lookup_table = jnp.concatenate(
        [features, pulled.reshape(wide_size * pull_slots, width)], axis=0
    )
    summed = features.astype(jnp.float32)
    for position in range(neighbours.shape[1]):
        picked = jnp.take(lookup_table, neighbours[:, position], axis=0)
        summed = summed + jnp.where(
            (position < degrees)[:, None], picked.astype(jnp.float32), jnp.float32(0.0)
        )
    agg = (summed / (degrees.astype(jnp.float32) + 1.0)[:, None]).astype(jnp.bfloat16)
    preact = jnp.dot(agg, weight, preferred_element_type=jnp.float32)
    sigma_value = jax.nn.sigmoid(preact)
    output_rows = (preact * sigma_value).astype(jnp.bfloat16)
    refreshed_store = jnp.take(output_rows, push_rows, axis=0)
    grad_pre = (
        cotangent.astype(jnp.float32) * sigma_value * (1.0 + preact * (1.0 - sigma_value))
    ).astype(jnp.bfloat16)
    scale_factor = 1.0 / math.sqrt(row_total * wide_size * narrow_size)
    own_part = lax.psum_scatter(
        lax.dot_general(
            agg, grad_pre, (((0,), (0,)), ((), ())), preferred_element_type=jnp.float32
        ),
        "wide",
        scatter_dimension=0,
        tiled=True,
    )
    grad_weight = lax.psum(own_part, "narrow")
    return (refreshed_store, grad_weight * scale_factor)


def solution(mesh):
    in_specs = (
        P(("wide", "narrow"), None),
        P(("wide", "narrow"), None),
        P(("wide", "narrow"), None),
        P(("wide", "narrow"), None),
        P(("wide", "narrow")),
        P(("wide", "narrow")),
        P(),
        P(("wide", "narrow"), None),
    )
    out_specs = (P(("wide", "narrow"), None), P("wide", None))
    return jax.shard_map(local, mesh=mesh, in_specs=in_specs, out_specs=out_specs, check_vma=False)
```

profile of v0, /device:TPU:6, one launch (start us, length us, event | category | flops | bytes accessed | tf_op | source)
XLA Modules:
  0.0 391.0 jit_solution(10582972597232274129)
XLA Ops:
  7.2 0.0 copy-start
  7.2 0.9 copy.12
  8.1 0.7 compare_and_fusion
  8.8 0.1 reshape.69
  8.9 0.1 copy.11
  9.0 3.8 gather_fusion
  12.9 0.0 copy-start.2
  12.9 0.0 copy-start.3
  12.9 1.1 bitcast_select_fusion
  14.0 0.0 copy-start.1
  14.0 14.5 %all-to-all-start = ((bf16[64,8,1024]{2,1,0:T(8,128)(2,1)}), bf16[64,8,1024]{2,1,0:T(8,128)(2,1)}, u32[]{:S(2)}, u32[]{:S(2)}) async-start(bf16[64,8,1024]{2,1,0:T(8,128)(2,1)} %bitcast_select_fusion), calls=%async_computation | async-start | bytes 2097152 | tf_op jit(solution)/shard_map/all_to_all | solution.py:18
  28.6 0.0 reduce-scatter.2.cloned.1.call-start
  28.6 0.0 copy-done.2
  28.8 0.0 copy-done.3
  29.0 28.4 %all-to-all-done = bf16[64,8,1024]{2,1,0:T(8,128)(2,1)} async-done(((bf16[64,8,1024]{2,1,0:T(8,128)(2,1)}), bf16[64,8,1024]{2,1,0:T(8,128)(2,1)}, u32[]{:S(2)}, u32[]{:S(2)}) %all-to-all-start) | async-done | bytes 1048608 | tf_op jit(solution)/shard_map/all_to_all | solution.py:18
  57.4 0.0 copy-done.1
  57.4 2.7 pad_maximum_fusion
  60.1 4.8 %gather_fusion.2 = bf16[512,1024]{1,0:T(8,128)(2,1)S(1)} fusion(bf16[1024,1024]{1,0:T(8,128)(2,1)} %pad_maximum_fusion, s32[1024]{0:T(1024)S(1)} %pad_clamp_fusion.8), kind=kCustom, calls=%fused_computation.clone | custom fusion | bytes 2099200 | tf_op jit(solution)/shard_map/jit(_take)/gather | solution.py:24
  64.9 5.4 %gather_fusion.3 = bf16[512,1024]{1,0:T(8,128)(2,1)} fusion(bf16[1024,1024]{1,0:T(8,128)(2,1)} %pad_maximum_fusion, s32[1024]{0:T(1024)S(1)} %pad_clamp_fusion.7), kind=kCustom, calls=%fused_computation.1.clone | custom fusion | bytes 2099200 | tf_op jit(solution)/shard_map/jit(_take)/gather | solution.py:24
  70.2 5.4 %gather_fusion.4 = bf16[512,1024]{1,0:T(8,128)(2,1)} fusion(bf16[1024,1024]{1,0:T(8,128)(2,1)} %pad_maximum_fusion, s32[1024]{0:T(1024)S(1)} %pad_clamp_fusion.6), kind=kCustom, calls=%fused_computation.2.clone | custom fusion | bytes 2099200 | tf_op jit(solution)/shard_map/jit(_take)/gather | solution.py:24
  75.6 5.3 %gather_fusion.5 = bf16[512,1024]{1,0:T(8,128)(2,1)} fusion(bf16[1024,1024]{1,0:T(8,128)(2,1)} %pad_maximum_fusion, s32[1024]{0:T(1024)S(1)} %pad_clamp_fusion.5), kind=kCustom, calls=%fused_computation.3.clone | custom fusion | bytes 2099200 | tf_op jit(solution)/shard_map/jit(_take)/gather | solution.py:24
  80.9 5.3 %gather_fusion.6 = bf16[512,1024]{1,0:T(8,128)(2,1)} fusion(bf16[1024,1024]{1,0:T(8,128)(2,1)} %pad_maximum_fusion, s32[1024]{0:T(1024)S(1)} %pad_clamp_fusion.4), kind=kCustom, calls=%fused_computation.4.clone | custom fusion | bytes 2099200 | tf_op jit(solution)/shard_map/jit(_take)/gather | solution.py:24
  86.3 5.3 %gather_fusion.7 = bf16[512,1024]{1,0:T(8,128)(2,1)} fusion(bf16[1024,1024]{1,0:T(8,128)(2,1)} %pad_maximum_fusion, s32[1024]{0:T(1024)S(1)} %pad_clamp_fusion.3), kind=kCustom, calls=%fused_computation.5.clone | custom fusion | bytes 2099200 | tf_op jit(solution)/shard_map/jit(_take)/gather | solution.py:24
  91.6 5.3 %gather_fusion.8 = bf16[512,1024]{1,0:T(8,128)(2,1)} fusion(bf16[1024,1024]{1,0:T(8,128)(2,1)} %pad_maximum_fusion, s32[1024]{0:T(1024)S(1)} %pad_clamp_fusion.2), kind=kCustom, calls=%fused_computation.6.clone | custom fusion | bytes 2099200 | tf_op jit(solution)/shard_map/jit(_take)/gather | solution.py:24
  97.0 5.3 %gather_fusion.9 = bf16[512,1024]{1,0:T(8,128)(2,1)} fusion(bf16[1024,1024]{1,0:T(8,128)(2,1)} %pad_maximum_fusion, s32[1024]{0:T(1024)S(1)} %pad_clamp_fusion.1), kind=kCustom, calls=%fused_computation.7.clone | custom fusion | bytes 2099200 | tf_op jit(solution)/shard_map/jit(_take)/gather | solution.py:24
  102.3 5.8 %divide_convert_fusion = bf16[512,1024]{1,0:T(8,128)(2,1)S(1)} fusion(bf16[512,1024]{1,0:T(8,128)(2,1)} %param.10, bf16[512,1024]{1,0:T(8,128)(2,1)} %gather_fusion.9, bf16[512,1024]{1,0:T(8,128)(2,1)} %gather_fusion.8, bf16[512,1024]{1,0:T(8,128)(2,1)} %gather_fusion.7, bf16[512,1024]{1,0:T(8,128)(2,1)} %gather_fusion.6, ...), kind=kLoop, calls=%fused_computation.14 | loop fusion | flops 18350080 | bytes 10496000 | tf_op jit(solution)/shard_map/convert_element_type | solution.py:28
  108.1 0.0 copy-done
  108.1 0.0 copy-start.5
  108.1 1.5 multiply_convert_fusion.1
  109.6 0.0 copy-done.5
  109.6 3.4 fusion
  113.0 0.0 copy-start.4
  113.0 0.0 reduce-scatter.2.cloned.1.call-update
  113.1 0.0 all-reduce.2.cloned.1.call-start
  113.1 0.6 copy-done.4
  113.7 2.0 gather_fusion.1
  115.7 154.8 %reduce-scatter.2.cloned.1.call-done = f32[16,1024]{1,0:T(8,128)} async-done(((f32[1024,1024]{1,0:T(8,128)}), f32[16,1024]{1,0:T(8,128)}) %reduce-scatter.2.cloned.1.call-update) | async-done | bytes 65552 | tf_op jit(solution)/shard_map/reduce_scatter | solution.py:37
  270.5 0.0 all-reduce.2.cloned.1.call-update
  270.5 2.0 broadcast_select_fusion
  272.5 110.2 %all-reduce.2.cloned.1.call-done = f32[16,1024]{1,0:T(8,128)} async-done(((f32[16,1024]{1,0:T(8,128)}), f32[16,1024]{1,0:T(8,128)}) %all-reduce.2.cloned.1.call-update) | async-done | bytes 65552 | tf_op jit(solution)/shard_map/psum | solution.py:45
  382.7 1.5 broadcast_multiply_fusion
  (28 shorter events, 0.2 us)
Async XLA Ops:
  7.2 100.9 %copy-start = (bf16[1024,1024]{1,0:T(8,128)(2,1)S(1)}, bf16[1024,1024]{1,0:T(8,128)(2,1)}, u32[]{:S(2)}) copy-start(bf16[1024,1024]{1,0:T(8,128)(2,1)} %param.16) | copy-start | bytes 6291460
  12.9 15.8 %copy-start.2 = (s32[512,8]{0,1:T(8,128)S(1)}, s32[512,8]{0,1:T(8,128)}, u32[]{:S(2)}) copy-start(s32[512,8]{0,1:T(8,128)} %param.13) | copy-start | bytes 49156
  12.9 16.0 %copy-start.3 = (s32[512]{0:T(512)S(1)}, s32[512]{0:T(512)}, u32[]{:S(2)}) copy-start(s32[512]{0:T(512)} %param.14) | copy-start | bytes 6148
  14.0 43.4 %copy-start.1 = (bf16[512,1024]{1,0:T(8,128)(2,1)S(1)}, bf16[512,1024]{1,0:T(8,128)(2,1)}, u32[]{:S(2)}) copy-start(bf16[512,1024]{1,0:T(8,128)(2,1)} %param.10) | copy-start | bytes 3145732
  14.0 43.3 %all-to-all-start = ((bf16[64,8,1024]{2,1,0:T(8,128)(2,1)}), bf16[64,8,1024]{2,1,0:T(8,128)(2,1)}, u32[]{:S(2)}, u32[]{:S(2)}) async-start(bf16[64,8,1024]{2,1,0:T(8,128)(2,1)} %bitcast_select_fusion), calls=%async_computation | async-start | bytes 2097152 | tf_op jit(solution)/shard_map/all_to_all | solution.py:18
  28.6 241.9 %reduce-scatter.2.cloned.1.call-start = ((), (), s32[]{:S(2)}) async-start(), calls=%async_computation.2 | async-start | bytes 4259840 | tf_op jit(solution)/shard_map/reduce_scatter | solution.py:37
  108.1 1.5 copy-start.5
  113.0 0.7 copy-start.4
  113.1 269.6 %all-reduce.2.cloned.1.call-start = ((), (), s32[]{:S(2)}) async-start(), calls=%async_computation.3 | async-start | bytes 131072 | tf_op jit(solution)/shard_map/psum | solution.py:45
Sparse Core Ops, SparseCore 0:
  113.2 157.2 reduce-scatter.1
  272.9 109.6 all-reduce.1
where the time goes:
time: 392 us; the launch traced here: 391 us
  waiting for transfers between devices  293 us (75%)
  local copies, waits for them, and re-layouts  49.7 us (13%)
  starting transfers between devices  14.6 us (4%)
  between operations  14.3 us (4%)
  other arithmetic  13.9 us (4%)
  matrix products  4.93 us (1%)
    reduce_scatter x1, waiting for transfers between devices, local(): lax.psum_scatter(lax.dot_general(agg, grad_pre, (((0,), (0,)), ((), ())),...  155 us
    psum x1, waiting for transfers between devices, local(): grad_weight = lax.psum(own_part, 'narrow')  110 us
    gather x8, local copies, waits for them, and re-layouts, local(): picked = jnp.take(lookup_table, neighbours[:, position], axis=0)  42.2 us
    all_to_all x1, waiting for transfers between devices, local(): lax.all_to_all(outgoing, 'wide', split_axis=0, concat_axis=0, tiled=True)  28.4 us
    all_to_all x1, starting transfers between devices, local(): lax.all_to_all(outgoing, 'wide', split_axis=0, concat_axis=0, tiled=True)  14.5 us
  transfers between devices with their start and end apart: 3, of which 3 were waited for; matrix products, arithmetic and copies ran while one was open for 1% of the time, Pallas kernels for 0%

commit v1 on v0

v1 whole, which is shorter than its diff:
```python
import functools
import math

import jax
import jax.numpy as jnp
from jax import lax
from jax.experimental import pallas as pl
from jax.experimental.pallas import tpu as pltpu
from jax.sharding import PartitionSpec as P

MESH = pl.DeviceIdType.MESH
F32 = jnp.float32
BF16 = jnp.bfloat16

NY, NX, NC = 8, 4, 2
NCH = 4
SCALE = 1.0 / math.sqrt(393216)


def iota(shape, dim):
    return lax.broadcasted_iota(jnp.int32, shape, dim)


def centre_out(k, half):
    return half + (1 - 2 * (k % 2)) * ((k + 1) // 2)


def kernel(
    features, store, serve_t, neigh_t, degrees, push, weight, cotangent,
    refreshed, grad_out,
    store_v, feat_v, weight_v, cot_v, outgoing, pulled, a_pull, acc, cols_v, push_v,
    agg, agg_t, agg_t_peer, out_v, dz, dz_peer, part,
    x_send, x_recv, y_send, y_recv, z_recv, refreshed_v,
    in_sem, pull_s, pull_r, core_s, core_r, xs, xr, ys, yr, zs, zr, out_sem,
):
    w = lax.axis_index("wide")
    n = lax.axis_index("narrow")
    nw, nz = NY * NX * NC, 12
    y, x, c = w // (NX * NC), (w // NC) % NX, w % NC
    rows, width = feat_v.shape
    cw = width // NCH

    loads = [
        pltpu.make_async_copy(src, dst, in_sem.at[i])
        for i, (src, dst) in enumerate(
            [(store, store_v), (features, feat_v), (weight, weight_v), (cotangent, cot_v)]
        )
    ]
    for load in loads:
        load.start()

    barrier = pltpu.get_barrier_semaphore()

    @pl.loop(1, nw)
    def _(j):
        pl.semaphore_signal(barrier, inc=1, device_id=((w + j) % nw, n), device_id_type=MESH)

    @pl.loop(1, nz)
    def _(j):
        pl.semaphore_signal(barrier, inc=1, device_id=(w, (n + j) % nz), device_id_type=MESH)

    slots = nw * 8
    tiled = jnp.tile(serve_t[...].astype(F32), (nw, 1))
    mine = iota((slots, nw), 1) == iota((slots, nw), 0) // 8
    wanted = jnp.sum(jnp.where(mine, tiled, 0.0), axis=1, keepdims=True)
    pick = (wanted.astype(jnp.int32) == iota((slots, store_v.shape[0]), 1)).astype(F32).astype(BF16)
    loads[0].wait()
    outgoing[...] = (
        jnp.dot(pick, store_v[...], preferred_element_type=F32).astype(BF16).reshape(nw, 8, width)
    )

    pl.semaphore_wait(barrier, nw - 1 + nz - 1)

    def pull_copy(j):
        dy = centre_out(j // (NX * NC), NY // 2)
        dx = centre_out((j // NC) % NX, NX // 2)
        dc = 1 - j % NC
        p = (((y + dy) % NY) * NX + (x + dx) % NX) * NC + (c + dc) % NC
        return p

    @pl.loop(0, nw - 1)
    def _(j):
        p = pull_copy(j)
        pltpu.make_async_remote_copy(
            src_ref=outgoing.at[p], dst_ref=pulled.at[w], send_sem=pull_s.at[p], recv_sem=pull_r.at[w],
            device_id=(p, n), device_id_type=MESH,
        ).start()

    pulled[w] = outgoing[w]
    deg = degrees[...]
    live = iota((8, rows), 0) < deg
    idx = jnp.where(live, neigh_t[...], -1).astype(F32)
    deg1 = jnp.broadcast_to(deg.astype(F32) + 1.0, (8, rows))
    pushed = jnp.concatenate([push[...].astype(F32)] * 2, axis=1)
    pushed = jnp.broadcast_to(pushed, (8, rows))
    stacked = jnp.concatenate([idx, deg1, pushed, jnp.zeros((104, rows), F32)], axis=0)
    cols_v[...] = stacked.T
    loads[1].wait()

    step = 64

    @pl.loop(0, rows // step)
    def _(b):
        r = pl.ds(pl.multiple_of(b * step, step), step)
        cols = cols_v[r, :].astype(jnp.int32)
        near = jnp.zeros((step, rows), F32)
        far = jnp.zeros((step, slots), F32)
        for k in range(8):
            col = cols[:, k : k + 1]
            near = near + (col == iota((step, rows), 1)).astype(F32)
            far = far + (col == iota((step, slots), 1) + rows).astype(F32)
        a_pull[r, :] = far.astype(BF16)
        acc[r, :] = feat_v[r, :].astype(F32) + jnp.dot(
            near.astype(BF16), feat_v[...], preferred_element_type=F32
        )

    push_v[...] = (
        (cols_v[0 : push_v.shape[0], 16:17].astype(jnp.int32) == iota(push_v.shape, 1)).astype(F32).astype(BF16)
    )
    loads[2].wait()
    loads[3].wait()

    @pl.loop(0, nw - 1)
    def _(j):
        p = pull_copy(j)
        pltpu.make_async_remote_copy(
            src_ref=outgoing.at[p], dst_ref=pulled.at[p], send_sem=pull_s.at[p], recv_sem=pull_r.at[p],
            device_id=(p, n), device_id_type=MESH,
        ).wait_recv()

    total = acc[...] + jnp.dot(
        a_pull[...], pulled[...].reshape(slots, width), preferred_element_type=F32
    )
    agg[...] = (total / cols_v[:, 8:9]).astype(BF16)
    agg_t[...] = agg[...].T.reshape(nw // NC, NC, 16, rows)

    other = (y * NX + x) * NC + 1 - c

    def core_copy(src, dst, i):
        return pltpu.make_async_remote_copy(
            src_ref=src, dst_ref=dst, send_sem=core_s.at[i], recv_sem=core_r.at[i],
            device_id=(other, n), device_id_type=MESH,
        )

    core = [core_copy(agg_t.at[:, 1 - c], agg_t_peer, NCH)]
    core[0].start()
    for h in range(NCH):
        at = pl.ds(h * cw, cw)
        z = jnp.dot(agg[...], weight_v[:, at], preferred_element_type=F32)
        s = jax.nn.sigmoid(z)
        out_v[:, at] = (z * s).astype(BF16)
        dz[h] = (cot_v[:, at].astype(F32) * s * (1.0 + z * (1.0 - s))).astype(BF16)
        copy = core_copy(dz.at[h], dz_peer.at[h], h)
        copy.start()
        core.append(copy)

    core[0].wait_recv()
    mine_t = agg_t[:, c].reshape(rows, rows)
    peer_t = agg_t_peer[...].reshape(rows, rows)

    def x_copy(h, d, there):
        px = (x + d) % NX
        return pltpu.make_async_remote_copy(
            src_ref=x_send.at[h, px], dst_ref=x_recv.at[h, x if there else px],
            send_sem=xs.at[h, px], recv_sem=xr.at[h, x if there else px],
            device_id=((y * NX + px) * NC + c, n), device_id_type=MESH,
        )

    def y_copy(h, d, there):
        py = (y + d) % NY
        return pltpu.make_async_remote_copy(
            src_ref=y_send.at[h, py], dst_ref=y_recv.at[h, y if there else py],
            send_sem=ys.at[h, py], recv_sem=yr.at[h, y if there else py],
            device_id=((py * NX + x) * NC + c, n), device_id_type=MESH,
        )

    def z_copy(h, d, there):
        pz = (n + d) % nz
        return pltpu.make_async_remote_copy(
            src_ref=z_recv.at[h, n], dst_ref=z_recv.at[h, n if there else pz],
            send_sem=zs.at[h, pz], recv_sem=zr.at[h, n if there else pz],
            device_id=(w, pz), device_id_type=MESH,
        )

    far_x, far_y = (2, 1, 3), (4, 3, 5, 2, 6, 1, 7)
    far_z = (6, 5, 7, 4, 8, 3, 9, 2, 10, 1, 11)
    for h in range(NCH):
        core[1 + h].wait_recv()
        g = jnp.dot(mine_t, dz[h], preferred_element_type=F32) + jnp.dot(
            peer_t, dz_peer[h], preferred_element_type=F32
        )
        part[h] = g.reshape(NY, NX, 16, cw)
        for k in range(NX):
            x_send[h, k] = part[h, :, k].astype(BF16)
        for d in far_x:
            x_copy(h, d, True).start()

    for h in range(NCH):
        at = pl.ds(h * cw, cw)
        refreshed_v[:, at] = jnp.dot(
            push_v[...], out_v[:, at], preferred_element_type=F32
        ).astype(BF16)
    store_back = pltpu.make_async_copy(refreshed_v, refreshed, out_sem)
    store_back.start()

    for h in range(NCH):
        for d in far_x:
            x_copy(h, d, False).wait_recv()
        total = part[h, :, x]
        for d in far_x:
            total = total + x_recv[h, (x + d) % NX].astype(F32)
        part[h, :, 0] = total
        y_send[h] = total.astype(BF16)
        for d in far_y:
            y_copy(h, d, True).start()

    for h in range(NCH):
        for d in far_y:
            y_copy(h, d, False).wait_recv()
        total = part[h, y, 0]
        for d in far_y:
            total = total + y_recv[h, (y + d) % NY].astype(F32)
        z_recv[h, n] = total.astype(BF16)
        for d in far_z:
            z_copy(h, d, True).start()

    for h in range(NCH):
        for d in far_z:
            z_copy(h, d, False).wait_recv()
        total = z_recv[h, 0].astype(F32)
        for k in range(1, nz):
            total = total + z_recv[h, k].astype(F32)
        grad_out[:, pl.ds(h * cw, cw)] = total * F32(SCALE)

    @pl.loop(0, nw - 1)
    def _(j):
        p = pull_copy(j)
        pltpu.make_async_remote_copy(
            src_ref=outgoing.at[p], dst_ref=pulled.at[p], send_sem=pull_s.at[p], recv_sem=pull_r.at[p],
            device_id=(p, n), device_id_type=MESH,
        ).wait_send()

    for copy in core:
        copy.wait_send()
    for h in range(NCH):
        for d in far_x:
            x_copy(h, d, True).wait_send()
        for d in far_y:
            y_copy(h, d, True).wait_send()
        for d in far_z:
            z_copy(h, d, True).wait_send()
    store_back.wait()


def local(features, stale_store, serve_rows, neighbours, degrees, push_rows, weight, cotangent):
    rows, width = features.shape
    stores = stale_store.shape[0]
    nw, nz = NY * NX * NC, 12
    cw = width // NCH
    any_, vmem = pl.BlockSpec(memory_space=pl.ANY), pl.BlockSpec(memory_space=pltpu.VMEM)
    dma = pltpu.SemaphoreType.DMA
    V = pltpu.VMEM
    return pl.pallas_call(
        kernel,
        out_shape=(
            jax.ShapeDtypeStruct((stores, width), BF16),
            jax.ShapeDtypeStruct((width // nw, width), F32),
        ),
        in_specs=[any_, any_, vmem, vmem, vmem, vmem, any_, any_],
        out_specs=(any_, vmem),
        scratch_shapes=[
            V((stores, width), BF16),
            V((rows, width), BF16),
            V((width, width), BF16),
            V((rows, width), BF16),
            V((nw, 8, width), BF16),
            V((nw, 8, width), BF16),
            V((rows, nw * 8), BF16),
            V((rows, width), F32),
            V((rows, 128), F32),
            V((stores, rows), BF16),
            V((rows, width), BF16),
            V((nw // NC, NC, 16, rows), BF16),
            V((nw // NC, 16, rows), BF16),
            V((rows, width), BF16),
            V((NCH, rows, cw), BF16),
            V((NCH, rows, cw), BF16),
            V((NCH, NY, NX, 16, cw), F32),
            V((NCH, NX, NY, 16, cw), BF16),
            V((NCH, NX, NY, 16, cw), BF16),
            V((NCH, NY, 16, cw), BF16),
            V((NCH, NY, 16, cw), BF16),
            V((NCH, nz, 16, cw), BF16),
            V((stores, width), BF16),
            dma((4,)),
            dma((nw,)),
            dma((nw,)),
            dma((NCH + 1,)),
            dma((NCH + 1,)),
            dma((NCH, NX)),
            dma((NCH, NX)),
            dma((NCH, NY)),
            dma((NCH, NY)),
            dma((NCH, nz)),
            dma((NCH, nz)),
            dma(()),
        ],
        compiler_params=pltpu.CompilerParams(
            collective_id=0, has_side_effects=True, vmem_limit_bytes=56 * 2**20
        ),
        cost_estimate=pl.CostEstimate(flops=6 * 10**9, bytes_accessed=6 * 2**20, transcendentals=2**20),
        name="sage",
    )(
        features, stale_store, serve_rows.T, neighbours.T, degrees.reshape(1, rows),
        push_rows.reshape(1, stores), weight, cotangent,
    )


def solution(mesh):
    both = P(("wide", "narrow"), None)
    flat = P(("wide", "narrow"))
    return jax.shard_map(
        local, mesh=mesh, in_specs=(both, both, both, both, flat, flat, P(), both),
        out_specs=(both, P("wide", None)), check_vma=False,
    )
```

time: 392 us -> 90.9 us (0.23)
  the two profiles are of different devices: /device:TPU:6 before, /device:TPU:1 now
where the time goes in v1:
time: 90.9 us; the launch traced here: 90.6 us
  Pallas kernels  86.6 us (95%)
  local copies, waits for them, and re-layouts  3.34 us (4%)
    pallas_call x1, Pallas kernels, local(): pl.pallas_call(kernel, out_shape=(jax.ShapeDtypeStruct((stores, width), B...  86.6 us
    unnamed x2, local copies, waits for them, and re-layouts  3.34 us

profile of v1, /device:TPU:1, one launch (start us, length us, event | category | flops | bytes accessed | tf_op | source)
XLA Modules:
  0.0 90.6 jit_solution(1671263178034849674)
XLA Ops:
  0.6 86.6 %sage.1 = (bf16[256,1024]{1,0:T(8,128)(2,1)}, f32[16,1024]{1,0:T(8,128)}) custom-call(bf16[512,1024]{1,0:T(8,128)(2,1)} %features.1, bf16[256,1024]{1,0:T(8,128)(2,1)} %store.1, s32[8,64]{1,0:T(8,128)} %bitcast.5, s32[8,512]{1,0:T(8,128)} %bitcast.4, s32[1,512]{1,0:T(1,128)} %bitcast.6, s32[1,256]{1,0:T(1,128)} %bitcast.7, bf16[1024,1024]{1,0:T(8,128)(2,1)} %weight.1, ...), custom_call_target="tpu_custom_call" | custom-call | flops 6000000000 | bytes 6291456 | tf_op jit(solution)/shard_map/sage/pallas_call | solution.py:263
  87.3 1.9 %copy.12 = bf16[256,1024]{1,0:T(8,128)(2,1)} copy(bf16[256,1024]{1,0:T(8,128)(2,1)} %get-tuple-element.4) | data formatting | bytes 1048576
  89.1 1.5 %copy.13 = f32[16,1024]{1,0:T(8,128)} copy(f32[16,1024]{1,0:T(8,128)} %get-tuple-element.5) | data formatting | bytes 131072

commit v2 on v1

v2 whole, which is shorter than its diff:
```python
import functools
import math

import jax
import jax.numpy as jnp
from jax import lax
from jax.experimental import pallas as pl
from jax.experimental.pallas import tpu as pltpu
from jax.sharding import PartitionSpec as P

MESH = pl.DeviceIdType.MESH
F32 = jnp.float32
BF16 = jnp.bfloat16

NY, NX, NC = 8, 4, 2
NCH = 4
FIRST = 2
SCALE = 1.0 / math.sqrt(393216)


def iota(shape, dim):
    return lax.broadcasted_iota(jnp.int32, shape, dim)


def kernel(
    features, store, serve_t, neigh_t, degrees, push, weight, cotangent,
    refreshed, grad_out,
    store_v, feat_v, weight_v, cot_v, pick, outgoing, staged, pulled, a_pull, acc, cols_v, push_v,
    agg, agg_t, agg_t_peer, out_v, dz, dz_peer, part,
    x_send, x_recv, y_send, y_recv, z_recv, refreshed_v,
    in_sem, pull_s, pull_r, relay_s, relay_r, core_s, core_r, xs, xr, ys, yr, zs, zr, out_sem,
):
    w = lax.axis_index("wide")
    n = lax.axis_index("narrow")
    nw, nz = NY * NX * NC, 12
    y, x, c = w // (NX * NC), (w // NC) % NX, w % NC
    rows, width = feat_v.shape
    cw = width // NCH

    loads = [
        pltpu.make_async_copy(src, dst, in_sem.at[i])
        for i, (src, dst) in enumerate(
            [(store, store_v), (features, feat_v), (weight, weight_v), (cotangent, cot_v)]
        )
    ]
    for load in loads:
        load.start()

    barrier = pltpu.get_barrier_semaphore()

    def at_y(d):
        return (((y + d) % NY * NX + x) * NC + c, n)

    def at_xc(dx, dc):
        return ((y * NX + (x + dx) % NX) * NC + (c + dc) % NC, n)

    far_x, far_y = (2, 1, 3), (4, 3, 5, 2, 6, 1, 7)
    far_z = (6, 5, 7, 4, 8, 3, 9, 2, 10, 1, 11)
    others = [at_y(d) for d in far_y] + [(w, (n + d) % nz) for d in far_z]
    others += [at_xc(dx, dc) for dx in range(NX) for dc in range(NC) if dx or dc]
    for device in others:
        pl.semaphore_signal(barrier, inc=1, device_id=device, device_id_type=MESH)

    slots = nw * 8
    tiled = jnp.tile(serve_t[...].astype(F32), (nw, 1))
    s = iota((slots, nw), 0)
    reader = ((s // 16) % NY * NX + s // (NY * 16)) * NC + (s // 8) % NC
    wanted = jnp.sum(jnp.where(iota((slots, nw), 1) == reader, tiled, 0.0), axis=1, keepdims=True)
    hot = wanted.astype(jnp.int32) == iota((slots, store_v.shape[0]), 1)
    pick[...] = hot.astype(F32).astype(BF16).reshape(pick.shape)
    loads[0].wait()

    rounds = (2, 1, 3, 0)

    def pull_copy(r, d, there):
        px, py = (x + rounds[r]) % NX, (y + d) % NY
        to = y if there else py
        return pltpu.make_async_remote_copy(
            src_ref=outgoing.at[px, py], dst_ref=staged.at[px, :, to],
            send_sem=pull_s.at[r, py], recv_sem=pull_r.at[r, to],
            device_id=at_y(d), device_id_type=MESH,
        )

    def relay_copy(dx, dc, there):
        px, pc = (x + dx) % NX, (c + dc) % NC
        to = x * NC + c if there else px * NC + pc
        return pltpu.make_async_remote_copy(
            src_ref=staged.at[px, pc], dst_ref=pulled.at[to],
            send_sem=relay_s.at[px * NC + pc], recv_sem=relay_r.at[to],
            device_id=at_xc(dx, dc), device_id_type=MESH,
        )

    def serve(r):
        px = (x + rounds[r]) % NX
        rows_out = jnp.dot(pick[px], store_v[...], preferred_element_type=F32).astype(BF16)
        outgoing[px] = rows_out.reshape(NY, NC, 8, width)
        if r == 0:
            pl.semaphore_wait(barrier, len(others))
        for d in far_y:
            pull_copy(r, d, True).start()
        staged[px, :, y] = outgoing[px, y]

    def relay(r):
        for d in far_y:
            pull_copy(r, d, False).wait_recv()
        dx = rounds[r]
        for dc in range(NC):
            if dx or dc:
                relay_copy(dx, dc, True).start()
            else:
                pulled[x * NC + c] = staged[x, c]

    for r in range(FIRST):
        serve(r)

    deg = degrees[...]
    live = iota((8, rows), 0) < deg
    idx = jnp.where(live, neigh_t[...], -1).astype(F32)
    deg1 = jnp.broadcast_to(deg.astype(F32) + 1.0, (8, rows))
    pushed = jnp.concatenate([push[...].astype(F32)] * 2, axis=1)
    pushed = jnp.broadcast_to(pushed, (8, rows))
    stacked = jnp.concatenate([idx, deg1, pushed, jnp.zeros((104, rows), F32)], axis=0)
    cols_v[...] = stacked.T
    loads[1].wait()

    step = 64
    at = iota((step, slots), 1)
    named = rows + (at // 8 % NY * (NX * NC) + at // (8 * NY)) * 8 + at % 8

    @pl.loop(0, rows // step)
    def _(b):
        r = pl.ds(pl.multiple_of(b * step, step), step)
        cols = cols_v[r, :].astype(jnp.int32)
        near = jnp.zeros((step, rows), F32)
        far = jnp.zeros((step, slots), F32)
        for k in range(8):
            col = cols[:, k : k + 1]
            near = near + (col == iota((step, rows), 1)).astype(F32)
            far = far + (col == named).astype(F32)
        a_pull[r, :] = far.astype(BF16)
        acc[r, :] = feat_v[r, :].astype(F32) + jnp.dot(
            near.astype(BF16), feat_v[...], preferred_element_type=F32
        )

    push_v[...] = (
        (cols_v[0 : push_v.shape[0], 16:17].astype(jnp.int32) == iota(push_v.shape, 1)).astype(F32).astype(BF16)
    )
    loads[2].wait()
    loads[3].wait()

    for r in range(NX):
        relay(r)
        if r + FIRST < NX:
            serve(r + FIRST)
    for dx in range(NX):
        for dc in range(NC):
            if dx or dc:
                relay_copy(dx, dc, False).wait_recv()

    total = acc[...] + jnp.dot(
        a_pull[...], pulled[...].reshape(slots, width), preferred_element_type=F32
    )
    agg[...] = (total / cols_v[:, 8:9]).astype(BF16)
    agg_t[...] = agg[...].T.reshape(nw // NC, NC, 16, rows)

    other = (y * NX + x) * NC + 1 - c

    def core_copy(src, dst, i):
        return pltpu.make_async_remote_copy(
            src_ref=src, dst_ref=dst, send_sem=core_s.at[i], recv_sem=core_r.at[i],
            device_id=(other, n), device_id_type=MESH,
        )

    core = [core_copy(dz.at[h], dz_peer.at[h], h) for h in range(NCH)]
    core.append(core_copy(agg_t.at[:, 1 - c], agg_t_peer, NCH))
    core[NCH].start()

    def x_copy(h, d, there):
        px = (x + d) % NX
        return pltpu.make_async_remote_copy(
            src_ref=x_send.at[h, px], dst_ref=x_recv.at[h, x if there else px],
            send_sem=xs.at[h, px], recv_sem=xr.at[h, x if there else px],
            device_id=((y * NX + px) * NC + c, n), device_id_type=MESH,
        )

    def y_copy(h, d, there):
        py = (y + d) % NY
        return pltpu.make_async_remote_copy(
            src_ref=y_send.at[h, py], dst_ref=y_recv.at[h, y if there else py],
            send_sem=ys.at[h, py], recv_sem=yr.at[h, y if there else py],
            device_id=((py * NX + x) * NC + c, n), device_id_type=MESH,
        )

    def z_copy(h, d, there):
        pz = (n + d) % nz
        return pltpu.make_async_remote_copy(
            src_ref=z_recv.at[h, n], dst_ref=z_recv.at[h, n if there else pz],
            send_sem=zs.at[h, pz], recv_sem=zr.at[h, n if there else pz],
            device_id=(w, pz), device_id_type=MESH,
        )

    def forward(h):
        at = pl.ds(h * cw, cw)
        z = jnp.dot(agg[...], weight_v[:, at], preferred_element_type=F32)
        s = jax.nn.sigmoid(z)
        dz[h] = (cot_v[:, at].astype(F32) * s * (1.0 + z * (1.0 - s))).astype(BF16)
        core[h].start()
        out_v[:, at] = (z * s).astype(BF16)

    def backward(h):
        if h == 0:
            core[NCH].wait_recv()
        g = jnp.dot(agg_t[:, c].reshape(rows, rows), dz[h], preferred_element_type=F32)
        core[h].wait_recv()
        g = g + jnp.dot(agg_t_peer[...].reshape(rows, rows), dz_peer[h], preferred_element_type=F32)
        part[h] = g.reshape(NY, NX, 16, cw)
        for k in range(NX):
            x_send[h, k] = part[h, :, k].astype(BF16)
        for d in far_x:
            x_copy(h, d, True).start()

    def after_x(h):
        for d in far_x:
            x_copy(h, d, False).wait_recv()
        total = part[h, :, x]
        for d in far_x:
            total = total + x_recv[h, (x + d) % NX].astype(F32)
        part[h, :, 0] = total
        y_send[h] = total.astype(BF16)
        for d in far_y:
            y_copy(h, d, True).start()

    def after_y(h):
        for d in far_y:
            y_copy(h, d, False).wait_recv()
        total = part[h, y, 0]
        for d in far_y:
            total = total + y_recv[h, (y + d) % NY].astype(F32)
        z_recv[h, n] = total.astype(BF16)
        for d in far_z:
            z_copy(h, d, True).start()

    def after_z(h):
        for d in far_z:
            z_copy(h, d, False).wait_recv()
        total = z_recv[h, 0].astype(F32)
        for k in range(1, nz):
            total = total + z_recv[h, k].astype(F32)
        grad_out[:, pl.ds(h * cw, cw)] = total * F32(SCALE)

    forward(0)
    forward(1)
    backward(0)
    forward(2)
    backward(1)
    forward(3)
    backward(2)
    backward(3)

    after_x(0)
    for h in range(NCH):
        at = pl.ds(h * cw, cw)
        refreshed_v[:, at] = jnp.dot(
            push_v[...], out_v[:, at], preferred_element_type=F32
        ).astype(BF16)
    store_back = pltpu.make_async_copy(refreshed_v, refreshed, out_sem)
    store_back.start()

    after_x(1)
    after_y(0)

    for r in range(NX):
        for d in far_y:
            pull_copy(r, d, True).wait_send()
    for dx in range(NX):
        for dc in range(NC):
            if dx or dc:
                relay_copy(dx, dc, True).wait_send()

    after_x(2)
    after_y(1)
    after_x(3)
    after_y(2)
    after_z(0)
    for copy in core:
        copy.wait_send()
    for h in range(NCH):
        for d in far_x:
            x_copy(h, d, True).wait_send()
    after_y(3)
    after_z(1)
    for h in range(NCH):
        for d in far_y:
            y_copy(h, d, True).wait_send()
    after_z(2)
    store_back.wait()
    after_z(3)
    for h in range(NCH):
        for d in far_z:
            z_copy(h, d, True).wait_send()


def finish(refreshed, grad, refreshed_out, grad_out, sem):
    copies = [
        pltpu.make_async_copy(refreshed, refreshed_out, sem.at[0]),
        pltpu.make_async_copy(grad, grad_out, sem.at[1]),
    ]
    for copy in copies:
        copy.start()
    for copy in copies:
        copy.wait()


def local(features, stale_store, serve_rows, neighbours, degrees, push_rows, weight, cotangent):
    rows, width = features.shape
    stores = stale_store.shape[0]
    nw, nz = NY * NX * NC, 12
    cw = width // NCH
    any_, vmem = pl.BlockSpec(memory_space=pl.ANY), pl.BlockSpec(memory_space=pltpu.VMEM)
    dma = pltpu.SemaphoreType.DMA
    V = pltpu.VMEM
    shapes = (
        jax.ShapeDtypeStruct((stores, width), BF16),
        jax.ShapeDtypeStruct((width // nw, width), F32),
    )
    made = pl.pallas_call(
        kernel,
        out_shape=shapes,
        in_specs=[any_, any_, vmem, vmem, vmem, vmem, any_, any_],
        out_specs=(any_, vmem),
        scratch_shapes=[
            V((stores, width), BF16),
            V((rows, width), BF16),
            V((width, width), BF16),
            V((rows, width), BF16),
            V((NX, NY * NC * 8, stores), BF16),
            V((NX, NY, NC, 8, width), BF16),
            V((NX, NC, NY, 8, width), BF16),
            V((NX * NC, NY, 8, width), BF16),
            V((rows, nw * 8), BF16),
            V((rows, width), F32),
            V((rows, 128), F32),
            V((stores, rows), BF16),
            V((rows, width), BF16),
            V((nw // NC, NC, 16, rows), BF16),
            V((nw // NC, 16, rows), BF16),
            V((rows, width), BF16),
            V((NCH, rows, cw), BF16),
            V((NCH, rows, cw), BF16),
            V((NCH, NY, NX, 16, cw), F32),
            V((NCH, NX, NY, 16, cw), BF16),
            V((NCH, NX, NY, 16, cw), BF16),
            V((NCH, NY, 16, cw), BF16),
            V((NCH, NY, 16, cw), BF16),
            V((NCH, nz, 16, cw), BF16),
            V((stores, width), BF16),
            dma((4,)),
            dma((NX, NY)),
            dma((NX, NY)),
            dma((NX * NC,)),
            dma((NX * NC,)),
            dma((NCH + 1,)),
            dma((NCH + 1,)),
            dma((NCH, NX)),
            dma((NCH, NX)),
            dma((NCH, NY)),
            dma((NCH, NY)),
            dma((NCH, nz)),
            dma((NCH, nz)),
            dma(()),
        ],
        compiler_params=pltpu.CompilerParams(
            collective_id=0, has_side_effects=True, vmem_limit_bytes=56 * 2**20
        ),
        cost_estimate=pl.CostEstimate(flops=6 * 10**9, bytes_accessed=6 * 2**20, transcendentals=2**20),
        name="sage",
    )(
        features, stale_store, serve_rows.T, neighbours.T, degrees.reshape(1, rows),
        push_rows.reshape(1, stores), weight, cotangent,
    )
    return pl.pallas_call(
        finish, out_shape=shapes, in_specs=[vmem, vmem], out_specs=(any_, any_),
        scratch_shapes=[dma((2,))], name="finish",
    )(*made)


def solution(mesh):
    both = P(("wide", "narrow"), None)
    flat = P(("wide", "narrow"))
    return jax.shard_map(
        local, mesh=mesh, in_specs=(both, both, both, both, flat, flat, P(), both),
        out_specs=(both, P("wide", None)), check_vma=False,
    )
```

time: 90.9 us -> 80.2 us (0.88)
  Pallas kernels: 86.6 us -> 78.7 us
  local copies, waits for them, and re-layouts: 3.34 us -> 0 us
    pallas_call x1 -> x2, Pallas kernels: 86.6 us -> 78.7 us  [the longest x1 76.9 us: local(): pl.pallas_call(kernel, out_shape=shapes, in_specs=[any_, any_, vmem, vmem...]
    unnamed x2 -> x0, local copies, waits for them, and re-layouts: 3.34 us -> none
where the time goes in v2:
time: 80.2 us; the launch traced here: 79.4 us
  Pallas kernels  78.7 us (98%)
    pallas_call x1, Pallas kernels, local(): pl.pallas_call(kernel, out_shape=shapes, in_specs=[any_, any_, vmem, vmem...  76.9 us
    pallas_call x1, Pallas kernels, local(): pl.pallas_call(finish, out_shape=shapes, in_specs=[vmem, vmem], out_specs...  1.86 us

profile of v2, /device:TPU:1, one launch (start us, length us, event | category | flops | bytes accessed | tf_op | source)
XLA Modules:
  0.0 79.4 jit_solution(10547478423168872644)
XLA Ops:
  0.6 76.9 %sage.1 = (bf16[256,1024]{1,0:T(8,128)(2,1)}, f32[16,1024]{1,0:T(8,128)}) custom-call(bf16[512,1024]{1,0:T(8,128)(2,1)} %features.1, bf16[256,1024]{1,0:T(8,128)(2,1)} %store.1, s32[8,64]{1,0:T(8,128)} %bitcast.5, s32[8,512]{1,0:T(8,128)} %bitcast.4, s32[1,512]{1,0:T(1,128)} %bitcast.6, s32[1,256]{1,0:T(1,128)} %bitcast.7, bf16[1024,1024]{1,0:T(8,128)(2,1)} %weight.1, ...), custom_call_target="tpu_custom_call" | custom-call | flops 6000000000 | bytes 6291456 | tf_op jit(solution)/shard_map/sage/pallas_call | solution.py:326
  77.5 1.9 %finish.1 = (bf16[256,1024]{1,0:T(8,128)(2,1)}, f32[16,1024]{1,0:T(8,128)}) custom-call(bf16[256,1024]{1,0:T(8,128)(2,1)} %get-tuple-element.4.refreshed, f32[16,1024]{1,0:T(8,128)} %get-tuple-element.5.grad), custom_call_target="tpu_custom_call" | custom-call | tf_op jit(solution)/shard_map/finish/pallas_call | solution.py:381

commit v3 on v2

--- a/solution.py
+++ b/solution.py
@@ -13,7 +13,10 @@
 BF16 = jnp.bfloat16
 
 NY, NX, NC = 8, 4, 2
-NCH = 4
+TILE = 128
+CHUNKS = ((0, 2), (2, 2), (4, 2), (6, 2))
+NCH = len(CHUNKS)
+SPLIT = (0, 1)
 FIRST = 2
 SCALE = 1.0 / math.sqrt(393216)
 
@@ -27,15 +30,34 @@
     refreshed, grad_out,
     store_v, feat_v, weight_v, cot_v, pick, outgoing, staged, pulled, a_pull, acc, cols_v, push_v,
     agg, agg_t, agg_t_peer, out_v, dz, dz_peer, part,
-    x_send, x_recv, y_send, y_recv, z_recv, refreshed_v,
-    in_sem, pull_s, pull_r, relay_s, relay_r, core_s, core_r, xs, xr, ys, yr, zs, zr, out_sem,
+    x_send, x_recv, y_send, y_recv, z_recv, tile_send, tile_recv, whole, refreshed_v,
+    in_sem, pull_s, pull_r, relay_s, relay_r, core_s, core_r, xs, xr, ys, yr, zs, zr, ss, sr, ws, wr, out_sem, ready,
 ):
     w = lax.axis_index("wide")
     n = lax.axis_index("narrow")
     nw, nz = NY * NX * NC, 12
     y, x, c = w // (NX * NC), (w // NC) % NX, w % NC
     rows, width = feat_v.shape
-    cw = width // NCH
+    tiles = width // TILE
+
+    barrier = pltpu.get_barrier_semaphore()
+
+    def at_y(d):
+        return (((y + d) % NY * NX + x) * NC + c, n)
+
+    def at_xc(dx, dc):
+        return ((y * NX + (x + dx) % NX) * NC + (c + dc) % NC, n)
+
+    far_x, far_y = (2, 1, 3), (4, 3, 5, 2, 6, 1, 7)
+    far_z = (6, 5, 7, 4, 8, 3, 9, 2, 10, 1, 11)
+    plane = [at_y(d) for d in far_y]
+    plane += [at_xc(dx, dc) for dx in range(NX) for dc in range(NC) if dx or dc]
+    for device in plane:
+        pl.semaphore_signal(barrier, inc=1, device_id=device, device_id_type=MESH)
+
+    @pl.loop(n + 1, nz)
+    def _(pz):
+        pl.semaphore_signal(barrier, inc=1, device_id=(w, pz), device_id_type=MESH)
 
     loads = [
         pltpu.make_async_copy(src, dst, in_sem.at[i])
@@ -45,21 +67,6 @@
     ]
     for load in loads:
         load.start()
-
-    barrier = pltpu.get_barrier_semaphore()
-
-    def at_y(d):
-        return (((y + d) % NY * NX + x) * NC + c, n)
-
-    def at_xc(dx, dc):
-        return ((y * NX + (x + dx) % NX) * NC + (c + dc) % NC, n)
-
-    far_x, far_y = (2, 1, 3), (4, 3, 5, 2, 6, 1, 7)
-    far_z = (6, 5, 7, 4, 8, 3, 9, 2, 10, 1, 11)
-    others = [at_y(d) for d in far_y] + [(w, (n + d) % nz) for d in far_z]
-    others += [at_xc(dx, dc) for dx in range(NX) for dc in range(NC) if dx or dc]
-    for device in others:
-        pl.semaphore_signal(barrier, inc=1, device_id=device, device_id_type=MESH)
 
     slots = nw * 8
     tiled = jnp.tile(serve_t[...].astype(F32), (nw, 1))
@@ -95,7 +102,7 @@
         rows_out = jnp.dot(pick[px], store_v[...], preferred_element_type=F32).astype(BF16)
         outgoing[px] = rows_out.reshape(NY, NC, 8, width)
         if r == 0:
-            pl.semaphore_wait(barrier, len(others))
+            pl.semaphore_wait(barrier, len(plane) + n)
         for d in far_y:
             pull_copy(r, d, True).start()
         staged[px, :, y] = outgoing[px, y]
@@ -112,6 +119,10 @@
 
     for r in range(FIRST):
         serve(r)
+
+    @pl.loop(0, n)
+    def _(pz):
+        pl.semaphore_signal(ready, inc=1, device_id=(w, pz), device_id_type=MESH)
 
     deg = degrees[...]
     live = iota((8, rows), 0) < deg
@@ -171,104 +182,180 @@
             device_id=(other, n), device_id_type=MESH,
         )
 
-    core = [core_copy(dz.at[h], dz_peer.at[h], h) for h in range(NCH)]
+    def columns(h):
+        t, k = CHUNKS[h]
+        return pl.ds(t * TILE, k * TILE)
+
+    def span(h):
+        return pl.ds(*CHUNKS[h])
+
+    core = [core_copy(dz.at[:, columns(h)], dz_peer.at[:, columns(h)], h) for h in range(NCH)]
     core.append(core_copy(agg_t.at[:, 1 - c], agg_t_peer, NCH))
     core[NCH].start()
 
     def x_copy(h, d, there):
         px = (x + d) % NX
-        return pltpu.make_async_remote_copy(
-            src_ref=x_send.at[h, px], dst_ref=x_recv.at[h, x if there else px],
-            send_sem=xs.at[h, px], recv_sem=xr.at[h, x if there else px],
-            device_id=((y * NX + px) * NC + c, n), device_id_type=MESH,
+        to = x if there else px
+        return pltpu.make_async_remote_copy(
+            src_ref=x_send.at[px, span(h)], dst_ref=x_recv.at[to, span(h)],
+            send_sem=xs.at[h, px], recv_sem=xr.at[h, to],
+            device_id=at_xc(d, 0), device_id_type=MESH,
         )
 
     def y_copy(h, d, there):
         py = (y + d) % NY
-        return pltpu.make_async_remote_copy(
-            src_ref=y_send.at[h, py], dst_ref=y_recv.at[h, y if there else py],
-            send_sem=ys.at[h, py], recv_sem=yr.at[h, y if there else py],
-            device_id=((py * NX + x) * NC + c, n), device_id_type=MESH,
+        to = y if there else py
+        return pltpu.make_async_remote_copy(
+            src_ref=y_send.at[py, span(h)], dst_ref=y_recv.at[to, span(h)],
+            send_sem=ys.at[h, py], recv_sem=yr.at[h, to],
+            device_id=at_y(d), device_id_type=MESH,
         )
 
     def z_copy(h, d, there):
         pz = (n + d) % nz
-        return pltpu.make_async_remote_copy(
-            src_ref=z_recv.at[h, n], dst_ref=z_recv.at[h, n if there else pz],
-            send_sem=zs.at[h, pz], recv_sem=zr.at[h, n if there else pz],
+        to = n if there else pz
+        return pltpu.make_async_remote_copy(
+            src_ref=z_recv.at[n, span(h)], dst_ref=z_recv.at[to, span(h)],
+            send_sem=zs.at[h, pz], recv_sem=zr.at[h, to],
             device_id=(w, pz), device_id_type=MESH,
         )
 
+    def owner(t):
+        return (t * 3) // 2
+
+    def split(h):
+        return range(CHUNKS[h][0], sum(CHUNKS[h]))
+
+    def tile_copy(t, sender):
+        return pltpu.make_async_remote_copy(
+            src_ref=tile_send.at[t], dst_ref=tile_recv.at[sender], send_sem=ss.at[t], recv_sem=sr.at[sender],
+            device_id=(w, owner(t)), device_id_type=MESH,
+        )
+
+    def whole_copy(t, pz):
+        return pltpu.make_async_remote_copy(
+            src_ref=whole.at[t], dst_ref=whole.at[t], send_sem=ws.at[pz], recv_sem=wr.at[t],
+            device_id=(w, pz), device_id_type=MESH,
+        )
+
     def forward(h):
-        at = pl.ds(h * cw, cw)
+        at = columns(h)
         z = jnp.dot(agg[...], weight_v[:, at], preferred_element_type=F32)
         s = jax.nn.sigmoid(z)
-        dz[h] = (cot_v[:, at].astype(F32) * s * (1.0 + z * (1.0 - s))).astype(BF16)
+        dz[:, at] = (cot_v[:, at].astype(F32) * s * (1.0 + z * (1.0 - s))).astype(BF16)
         core[h].start()
         out_v[:, at] = (z * s).astype(BF16)
 
     def backward(h):
+        at = columns(h)
         if h == 0:
             core[NCH].wait_recv()
-        g = jnp.dot(agg_t[:, c].reshape(rows, rows), dz[h], preferred_element_type=F32)
+        g = jnp.dot(agg_t[:, c].reshape(rows, rows), dz[:, at], preferred_element_type=F32)
         core[h].wait_recv()
-        g = g + jnp.dot(agg_t_peer[...].reshape(rows, rows), dz_peer[h], preferred_element_type=F32)
-        part[h] = g.reshape(NY, NX, 16, cw)
-        for k in range(NX):
-            x_send[h, k] = part[h, :, k].astype(BF16)
+        g = g + jnp.dot(agg_t_peer[...].reshape(rows, rows), dz_peer[:, at], preferred_element_type=F32)
+        for i, t in enumerate(split(h)):
+            tile = g[:, i * TILE : (i + 1) * TILE].reshape(NY, NX, 16, TILE)
+            part[t] = tile
+            for k in range(NX):
+                x_send[k, t] = tile[:, k].astype(BF16)
         for d in far_x:
             x_copy(h, d, True).start()
 
     def after_x(h):
         for d in far_x:
             x_copy(h, d, False).wait_recv()
-        total = part[h, :, x]
-        for d in far_x:
-            total = total + x_recv[h, (x + d) % NX].astype(F32)
-        part[h, :, 0] = total
-        y_send[h] = total.astype(BF16)
+        for t in split(h):
+            total = part[t, :, x]
+            for d in far_x:
+                total = total + x_recv[(x + d) % NX, t].astype(F32)
+            part[t, :, 0] = total
+            for k in range(NY):
+                y_send[k, t] = total[k].astype(BF16)
         for d in far_y:
             y_copy(h, d, True).start()
 
     def after_y(h):
         for d in far_y:
             y_copy(h, d, False).wait_recv()
-        total = part[h, y, 0]
-        for d in far_y:
-            total = total + y_recv[h, (y + d) % NY].astype(F32)
-        z_recv[h, n] = total.astype(BF16)
-        for d in far_z:
-            z_copy(h, d, True).start()
+        for t in split(h):
+            total = part[t, y, 0]
+            for d in far_y:
+                total = total + y_recv[(y + d) % NY, t].astype(F32)
+            if h not in SPLIT:
+                z_recv[n, t] = total.astype(BF16)
+                continue
+            tile_send[t] = total.astype(BF16)
+
+            @pl.when(n == owner(t))
+            def _():
+                tile_recv[n] = tile_send[t]
+
+            @pl.when(n != owner(t))
+            def _():
+                tile_copy(t, n).start()
+
+        if h not in SPLIT:
+            for d in far_z:
+                z_copy(h, d, True).start()
+
+    def after_split(h):
+        for t in split(h):
+
+            @pl.when(n == owner(t))
+            def _():
+                @pl.loop(1, nz)
+                def _(d):
+                    tile_copy(t, (n + d) % nz).wait_recv()
+
+                total = tile_recv[0].astype(F32)
+                for k in range(1, nz):
+                    total = total + tile_recv[k].astype(F32)
+                whole[t] = total * F32(SCALE)
+                for d in far_z:
+                    whole_copy(t, (n + d) % nz).start()
 
     def after_z(h):
-        for d in far_z:
-            z_copy(h, d, False).wait_recv()
-        total = z_recv[h, 0].astype(F32)
-        for k in range(1, nz):
-            total = total + z_recv[h, k].astype(F32)
-        grad_out[:, pl.ds(h * cw, cw)] = total * F32(SCALE)
+        if h not in SPLIT:
+            for d in far_z:
+                z_copy(h, d, False).wait_recv()
+        for t in split(h):
+            if h in SPLIT:
+
+                @pl.when(n != owner(t))
+                def _():
+                    whole_copy(t, n).wait_recv()
+
+                total = whole[t]
+            else:
+                total = z_recv[0, t].astype(F32)
+                for k in range(1, nz):
+                    total = total + z_recv[k, t].astype(F32)
+                total = total * F32(SCALE)
+            grad_out[:, pl.ds(t * TILE, TILE)] = total
 
     forward(0)
-    forward(1)
-    backward(0)
-    forward(2)
-    backward(1)
-    forward(3)
-    backward(2)
-    backward(3)
-
-    after_x(0)
+    for h in range(1, NCH):
+        forward(h)
+        backward(h - 1)
+    backward(NCH - 1)
+
     for h in range(NCH):
-        at = pl.ds(h * cw, cw)
+        at = columns(h)
         refreshed_v[:, at] = jnp.dot(
             push_v[...], out_v[:, at], preferred_element_type=F32
         ).astype(BF16)
+        if h == 0:
+            after_x(0)
     store_back = pltpu.make_async_copy(refreshed_v, refreshed, out_sem)
     store_back.start()
-
-    after_x(1)
-    after_y(0)
-
+    @pl.when(n < nz - 1)
+    def _():
+        pl.semaphore_wait(ready, nz - 1 - n)
+
+
+    for h in range(1, NCH):
+        after_x(h)
+        after_y(h - 1)
     for r in range(NX):
         for d in far_y:
             pull_copy(r, d, True).wait_send()
@@ -276,28 +363,35 @@
         for dc in range(NC):
             if dx or dc:
                 relay_copy(dx, dc, True).wait_send()
-
-    after_x(2)
-    after_y(1)
-    after_x(3)
-    after_y(2)
-    after_z(0)
+    after_y(NCH - 1)
+    for h in SPLIT:
+        after_split(h)
     for copy in core:
         copy.wait_send()
     for h in range(NCH):
         for d in far_x:
             x_copy(h, d, True).wait_send()
-    after_y(3)
-    after_z(1)
+        for d in far_y:
+            y_copy(h, d, True).wait_send()
+    store_back.wait()
     for h in range(NCH):
-        for d in far_y:
-            y_copy(h, d, True).wait_send()
-    after_z(2)
-    store_back.wait()
-    after_z(3)
+        after_z(h)
     for h in range(NCH):
-        for d in far_z:
-            z_copy(h, d, True).wait_send()
+        if h not in SPLIT:
+            for d in far_z:
+                z_copy(h, d, True).wait_send()
+            continue
+        for t in split(h):
+
+            @pl.when(n != owner(t))
+            def _():
+                tile_copy(t, n).wait_send()
+
+            @pl.when(n == owner(t))
+            def _():
+                @pl.loop(1, nz)
+                def _(d):
+                    whole_copy(t, (n + d) % nz).wait_send()
 
 
 def finish(refreshed, grad, refreshed_out, grad_out, sem):
@@ -315,7 +409,7 @@
     rows, width = features.shape
     stores = stale_store.shape[0]
     nw, nz = NY * NX * NC, 12
-    cw = width // NCH
+    tiles = width // TILE
     any_, vmem = pl.BlockSpec(memory_space=pl.ANY), pl.BlockSpec(memory_space=pltpu.VMEM)
     dma = pltpu.SemaphoreType.DMA
     V = pltpu.VMEM
@@ -345,14 +439,17 @@
             V((nw // NC, NC, 16, rows), BF16),
             V((nw // NC, 16, rows), BF16),
             V((rows, width), BF16),
-            V((NCH, rows, cw), BF16),
-            V((NCH, rows, cw), BF16),
-            V((NCH, NY, NX, 16, cw), F32),
-            V((NCH, NX, NY, 16, cw), BF16),
-            V((NCH, NX, NY, 16, cw), BF16),
-            V((NCH, NY, 16, cw), BF16),
-            V((NCH, NY, 16, cw), BF16),
-            V((NCH, nz, 16, cw), BF16),
+            V((rows, width), BF16),
+            V((rows, width), BF16),
+            V((tiles, NY, NX, 16, TILE), F32),
+            V((NX, tiles, NY, 16, TILE), BF16),
+            V((NX, tiles, NY, 16, TILE), BF16),
+            V((NY, tiles, 16, TILE), BF16),
+            V((NY, tiles, 16, TILE), BF16),
+            V((nz, tiles, 16, TILE), BF16),
+            V((tiles, 16, TILE), BF16),
+            V((nz, 16, TILE), BF16),
+            V((tiles, 16, TILE), F32),
             V((stores, width), BF16),
             dma((4,)),
             dma((NX, NY)),
@@ -367,7 +464,12 @@
             dma((NCH, NY)),
             dma((NCH, nz)),
             dma((NCH, nz)),
+            dma((tiles,)),
+            dma((nz,)),
+            dma((nz,)),
+            dma((tiles,)),
             dma(()),
+            pltpu.SemaphoreType.REGULAR,
         ],
         compiler_params=pltpu.CompilerParams(
             collective_id=0, has_side_effects=True, vmem_limit_bytes=56 * 2**20

time: 80.2 us -> 79 us (0.985)
  no operation moved by 1% of the time
where the time goes in v3:
time: 79 us; the launch traced here: 78.7 us
  Pallas kernels  78 us (99%)
    pallas_call x1, Pallas kernels, local(): pl.pallas_call(kernel, out_shape=shapes, in_specs=[any_, any_, vmem, vmem...  76.2 us
    pallas_call x1, Pallas kernels, local(): pl.pallas_call(finish, out_shape=shapes, in_specs=[vmem, vmem], out_specs...  1.86 us

profile of v3, /device:TPU:1, one launch (start us, length us, event | category | flops | bytes accessed | tf_op | source)
XLA Modules:
  0.0 78.7 jit_solution(7444954228619657824)
XLA Ops:
  0.6 76.2 %sage.1 = (bf16[256,1024]{1,0:T(8,128)(2,1)}, f32[16,1024]{1,0:T(8,128)}) custom-call(bf16[512,1024]{1,0:T(8,128)(2,1)} %features.1, bf16[256,1024]{1,0:T(8,128)(2,1)} %store.1, s32[8,64]{1,0:T(8,128)} %bitcast.5, s32[8,512]{1,0:T(8,128)} %bitcast.4, s32[1,512]{1,0:T(1,128)} %bitcast.6, s32[1,256]{1,0:T(1,128)} %bitcast.7, bf16[1024,1024]{1,0:T(8,128)(2,1)} %weight.1, ...), custom_call_target="tpu_custom_call" | custom-call | flops 6000000000 | bytes 6291456 | tf_op jit(solution)/shard_map/sage/pallas_call | solution.py:420
  76.8 1.9 %finish.1 = (bf16[256,1024]{1,0:T(8,128)(2,1)}, f32[16,1024]{1,0:T(8,128)}) custom-call(bf16[256,1024]{1,0:T(8,128)(2,1)} %get-tuple-element.4.refreshed, f32[16,1024]{1,0:T(8,128)} %get-tuple-element.5.grad), custom_call_target="tpu_custom_call" | custom-call | tf_op jit(solution)/shard_map/finish/pallas_call | solution.py:483

commit v4 on v3

--- a/solution.py
+++ b/solution.py
@@ -83,7 +83,7 @@
         px, py = (x + rounds[r]) % NX, (y + d) % NY
         to = y if there else py
         return pltpu.make_async_remote_copy(
-            src_ref=outgoing.at[px, py], dst_ref=staged.at[px, :, to],
+            src_ref=outgoing.at[px, py], dst_ref=staged.at[px, to],
             send_sem=pull_s.at[r, py], recv_sem=pull_r.at[r, to],
             device_id=at_y(d), device_id_type=MESH,
         )
@@ -92,7 +92,7 @@
         px, pc = (x + dx) % NX, (c + dc) % NC
         to = x * NC + c if there else px * NC + pc
         return pltpu.make_async_remote_copy(
-            src_ref=staged.at[px, pc], dst_ref=pulled.at[to],
+            src_ref=staged.at[px, :, pc], dst_ref=pulled.at[to],
             send_sem=relay_s.at[px * NC + pc], recv_sem=relay_r.at[to],
             device_id=at_xc(dx, dc), device_id_type=MESH,
         )
@@ -105,7 +105,7 @@
             pl.semaphore_wait(barrier, len(plane) + n)
         for d in far_y:
             pull_copy(r, d, True).start()
-        staged[px, :, y] = outgoing[px, y]
+        staged[px, y] = outgoing[px, y]
 
     def relay(r):
         for d in far_y:
@@ -115,7 +115,7 @@
             if dx or dc:
                 relay_copy(dx, dc, True).start()
             else:
-                pulled[x * NC + c] = staged[x, c]
+                pulled[x * NC + c] = staged[x, :, c]
 
     for r in range(FIRST):
         serve(r)
@@ -221,7 +221,7 @@
         )
 
     def owner(t):
-        return (t * 3) // 2
+        return t
 
     def split(h):
         return range(CHUNKS[h][0], sum(CHUNKS[h]))
@@ -429,7 +429,7 @@
             V((rows, width), BF16),
             V((NX, NY * NC * 8, stores), BF16),
             V((NX, NY, NC, 8, width), BF16),
-            V((NX, NC, NY, 8, width), BF16),
+            V((NX, NY, NC, 8, width), BF16),
             V((NX * NC, NY, 8, width), BF16),
             V((rows, nw * 8), BF16),
             V((rows, width), F32),

time: 79 us -> 79 us (level)
  no operation moved by 1% of the time
where the time goes in v4:
time: 79 us; the launch traced here: 78.8 us
  Pallas kernels  78.2 us (99%)
    pallas_call x1, Pallas kernels, local(): pl.pallas_call(kernel, out_shape=shapes, in_specs=[any_, any_, vmem, vmem...  76.3 us
    pallas_call x1, Pallas kernels, local(): pl.pallas_call(finish, out_shape=shapes, in_specs=[vmem, vmem], out_specs...  1.86 us

profile of v4, /device:TPU:1, one launch (start us, length us, event | category | flops | bytes accessed | tf_op | source)
XLA Modules:
  0.0 78.8 jit_solution(1285095012192090260)
XLA Ops:
  0.6 76.3 %sage.1 = (bf16[256,1024]{1,0:T(8,128)(2,1)}, f32[16,1024]{1,0:T(8,128)}) custom-call(bf16[512,1024]{1,0:T(8,128)(2,1)} %features.1, bf16[256,1024]{1,0:T(8,128)(2,1)} %store.1, s32[8,64]{1,0:T(8,128)} %bitcast.5, s32[8,512]{1,0:T(8,128)} %bitcast.4, s32[1,512]{1,0:T(1,128)} %bitcast.6, s32[1,256]{1,0:T(1,128)} %bitcast.7, bf16[1024,1024]{1,0:T(8,128)(2,1)} %weight.1, ...), custom_call_target="tpu_custom_call" | custom-call | flops 6000000000 | bytes 6291456 | tf_op jit(solution)/shard_map/sage/pallas_call | solution.py:420
  77.0 1.9 %finish.1 = (bf16[256,1024]{1,0:T(8,128)(2,1)}, f32[16,1024]{1,0:T(8,128)}) custom-call(bf16[256,1024]{1,0:T(8,128)(2,1)} %get-tuple-element.4.refreshed, f32[16,1024]{1,0:T(8,128)} %get-tuple-element.5.grad), custom_call_target="tpu_custom_call" | custom-call | tf_op jit(solution)/shard_map/finish/pallas_call | solution.py:483
